TPU v7x, 512 devices: a whole 4x8x8 slice. The times are simulated.
512 devices in a mesh: dp: 64 (over z_hi, y, core), mp: 8 (over z_lo, x).
Axes of the slice: x: 4, y: 8, z: 8 (z_hi: 4, z_lo: 2; z = z_hi * 2 + z_lo), core: 2. Of those that a mesh axis runs over, the one named last changes fastest.
Arguments:
- hidden: bfloat16 [40960, 14336], P('dp', 'mp'), may hold values from -6 to 6
- out_grad: bfloat16 [40960, 512], P('dp'), may hold values from -0.23632812 to 0.23632812
- master: float32 [14336, 512], P(('mp', 'dp')), may hold values from -0.03 to 0.03
- moment_one: float32 [14336, 512], P(('mp', 'dp')), may hold values from -0.12 to 0.12
- moment_two: float32 [14336, 512], P(('mp', 'dp')), may hold values from 0.0001 to 0.001
- sign_flips: int32 [512], replicated, may hold values from -1 to 1, as said below
- step_count: int32 [1], replicated, may hold values from 1 to 8
Outputs:
- weights: bfloat16 [14336, 512], P('mp')
- update: float32 [14336, 512], P(('mp', 'dp'))
Inputs may be any that keep to these rules, and one draw needn't show every extreme that they name: `sign_flips`: each entry is -1 or 1.
All inputs are finite; a program needn't handle non-finite values.
Results may differ from a plain program's by a relative error of at most 0.007.
Values may be sent and summed in bfloat16 or wider, within the bound.
No kernel may reach another device: no remote copies, remote signals or barrier semaphores. Data moves between devices by JAX's collectives and lax.ppermute only.
A program may use at most 64 MiB of HBM per device.

v0:
```python
import jax
import jax.numpy as jnp
from jax import lax
from jax.sharding import PartitionSpec as P


def hadamard_table(order):
    table = jnp.ones((1, 1), jnp.float32)
    while table.shape[0] < order:
        table = jnp.concatenate(
            [jnp.concatenate([table, table], axis=1), jnp.concatenate([table, -table], axis=1)],
            axis=0,
        )
    return table


def local(hidden, out_grad, master, moment_one, moment_two, sign_flips, step_count):
    columns = out_grad.shape[1]
    factor = columns ** (-0.5)
    table = hadamard_table(columns) * factor
    table_half = table.astype(jnp.bfloat16)
    flips_half = sign_flips.astype(jnp.bfloat16)
    flips_full = sign_flips.astype(jnp.float32)
    replicas = lax.axis_size("dp")
    partial_value = lax.dot_general(
        hidden, out_grad, (((0,), (0,)), ((), ())), preferred_element_type=jnp.float32
    )
    signed = partial_value.astype(jnp.bfloat16) * flips_half[None, :]
    rotated = jnp.dot(signed, table_half, preferred_element_type=jnp.float32).astype(jnp.bfloat16)
    summed = lax.psum_scatter(rotated.astype(jnp.float32), "dp", scatter_dimension=0, tiled=True)
    gradient = summed / replicas
    steps_done = step_count[0].astype(jnp.float32)
    first = 0.9 * moment_one + 0.1 * gradient
    second = 0.95 * moment_two + 0.05 * gradient * gradient
    first_hat = first / (1.0 - jnp.power(jnp.float32(0.9), steps_done))
    second_hat = second / (1.0 - jnp.power(jnp.float32(0.95), steps_done))
    direction = first_hat / (jnp.sqrt(second_hat) + 1e-08)
    update = (
        jnp.dot(direction, table, precision=lax.Precision.HIGHEST) * flips_full[None, :]
        + 0.1 * master
    )
    own_weights = (master - 0.0003 * update).astype(jnp.bfloat16)
    weights = lax.all_gather(own_weights, "dp", axis=0, tiled=True)
    return (weights, update)


def solution(mesh):
    return jax.shard_map(
        local,
        mesh=mesh,
        in_specs=(
            P("dp", "mp"),
            P("dp", None),
            P(("mp", "dp"), None),
            P(("mp", "dp"), None),
            P(("mp", "dp"), None),
            P(),
            P(),
        ),
        out_specs=(P("mp", None), P(("mp", "dp"), None)),
        check_vma=False,
    )
```

profile of v0, /device:TPU:1, one launch (start us, length us, event | category | flops | bytes accessed | tf_op | source)
XLA Modules:
  0.0 335.1 jit_solution(12141799376921735877)
XLA Ops:
  7.2 0.0 copy-start
  7.2 0.0 all-gather.3.cloned.1.call-start
  7.2 0.9 fusion.33
  8.1 0.8 copy-done
  8.8 5.6 %fusion.1 = f32[1792,512]{1,0:T(8,128)} fusion(bf16[512,512]{1,0:T(8,128)(2,1)} %constant.26.clone.1, bf16[640,1792]{1,0:T(8,128)(2,1)S(1)} %copy-done, bf16[640,512]{1,0:T(8,128)(2,1)} %param.8, bf16[512]{0:T(512)(128)(2,1)S(1)} %get-tuple-element.3), kind=kOutput, calls=%fused_computation.1 | convolution fusion | flops 2117599232 | bytes 7144448 | tf_op jit(solution)/shard_map/dot_general | solution.py:29
  14.5 178.2 %fusion = f32[32,512]{1,0:T(8,128)S(1)} fusion(f32[1792,512]{1,0:T(8,128)} %fusion.1), kind=kCustom, calls=%all-reduce-scatter | all-reduce-scatter fusion | flops 1048577 | bytes 3737600
  192.7 1.3 collective-permute-start.6
  194.0 1.3 collective-permute-start.5
  195.3 1.3 collective-permute-start.7
  196.6 1.9 collective-permute-start.4
  198.5 10.8 %collective-permute-start.3 = (f32[32,512]{1,0:T(8,128)S(1)}, f32[32,512]{1,0:T(8,128)}, u32[]{:S(2)}, u32[]{:S(2)}) collective-permute-start(f32[32,512]{1,0:T(8,128)S(1)} %fusion), channel_id=1, source_target_pairs={{0,32},{8,40},{16,48},{24,56},{32,64},{40,72},{48,80},{56,88},{64,... | collective-permute-start | bytes 196616
  209.3 1.9 collective-permute-start.2
  211.2 0.0 collective-permute-done.6
  211.2 8.3 %collective-permute-start.1 = (f32[32,512]{1,0:T(8,128)S(1)}, f32[32,512]{1,0:T(8,128)}, u32[]{:S(2)}, u32[]{:S(2)}) collective-permute-start(f32[32,512]{1,0:T(8,128)S(1)} %fusion), channel_id=1, source_target_pairs={{0,16},{8,24},{16,32},{24,40},{32,48},{40,56},{48,64},{56,72},{64,... | collective-permute-start | bytes 196616
  219.5 2.2 collective-permute-start
  222.4 1.3 dynamic-slice.4
  224.3 0.0 collective-permute-done.4
  224.4 13.2 %concatenate = f32[284,512]{1,0:T(8,128)} concatenate(f32[28,512]{1,0:T(8,128)} %copy-done.7, f32[32,512]{1,0:T(8,128)} %copy-done.5, f32[32,512]{1,0:T(8,128)} %copy-done.6, f32[32,512]{1,0:T(8,128)} %collective-permute-done.4, f32[32,512]{1,0:T(8,128)} %collective-permute-done.3, f32[32,512]{1,0:T(8,128)} %collective-permute-done.2, f32[32,512]{1,0:T(8,128)} %collective-permute-done.1, ...), dimensions={0} | concatenate | bytes 1163264
  237.6 1.6 fusion.3
  239.2 0.0 copy-start.3
  239.3 0.6 fusion.17
  239.9 0.0 all-gather.3.cloned.1.call-update
  239.9 84.6 %all-gather.3.cloned.1.call-done = bf16[64,28,512]{2,1,0:T(8,128)(2,1)} async-done(((bf16[1,28,512]{2,1,0:T(8,128)(2,1)}), bf16[64,28,512]{2,1,0:T(8,128)(2,1)}) %all-gather.3.cloned.1.call-update) | async-done | bytes 1835024 | tf_op jit(solution)/shard_map/all_gather | solution.py:43
  324.5 3.7 %reshape.16 = bf16[1792,512]{1,0:T(8,128)(2,1)} reshape(bf16[64,28,512]{2,1,0:T(8,128)(2,1)} %all-gather.3.cloned.1.call-done) | data formatting | bytes 3670016
  (20 shorter events, 0.0 us)
Async XLA Ops:
  7.2 1.7 copy-start
  7.2 317.4 %all-gather.3.cloned.1.call-start = ((), (), s32[]{:S(2)}) async-start(), calls=%async_computation | async-start | bytes 2129920 | tf_op jit(solution)/shard_map/all_gather | solution.py:43
  14.5 223.1 %copy-start.1 = (f32[512,512]{1,0:T(8,128)S(1)}, f32[512,512]{1,0:T(8,128)}, u32[]{:S(2)}) copy-start(f32[512,512]{1,0:T(8,128)} %constant.35.clone.1) | copy-start | bytes 3145732
  14.5 223.1 %copy-start.2 = (f32[28,512]{1,0:T(8,128)S(1)}, f32[28,512]{1,0:T(8,128)}, u32[]{:S(2)}) copy-start(f32[28,512]{1,0:T(8,128)} %param.9) | copy-start | bytes 172036
  14.5 223.1 %copy-start.4 = (f32[28,512]{1,0:T(8,128)S(1)}, f32[28,512]{1,0:T(8,128)}, u32[]{:S(2)}) copy-start(f32[28,512]{1,0:T(8,128)} %param.11) | copy-start | bytes 172036
  192.7 18.5 %collective-permute-start.6 = (f32[32,512]{1,0:T(8,128)S(1)}, f32[32,512]{1,0:T(8,128)S(1)}, u32[]{:S(2)}, u32[]{:S(2)}) collective-permute-start(f32[32,512]{1,0:T(8,128)S(1)} %fusion), channel_id=1, source_target_pairs={{0,56},{8,64},{16,72},{24,80},{32,88},{40,96},{48,104},{56,112},{6... | collective-permute-start | bytes 196616
  194.0 25.5 %collective-permute-start.5 = (f32[32,512]{1,0:T(8,128)S(1)}, f32[32,512]{1,0:T(8,128)S(1)}, u32[]{:S(2)}, u32[]{:S(2)}) collective-permute-start(f32[32,512]{1,0:T(8,128)S(1)} %fusion), channel_id=1, source_target_pairs={{0,48},{8,56},{16,64},{24,72},{32,80},{40,88},{48,96},{56,104},{64... | collective-permute-start | bytes 196616
  195.3 14.0 %collective-permute-start.7 = (f32[28,512]{1,0:T(8,128)S(1)}, f32[28,512]{1,0:T(8,128)S(1)}, u32[]{:S(2)}, u32[]{:S(2)}) collective-permute-start(f32[28,512]{1,0:T(8,128)S(1)} %slice), channel_id=1, source_target_pairs={{0,64},{8,72},{16,80},{24,88},{32,96},{40,104},{48,112},{56,120},{... | collective-permute-start | bytes 172040
  196.6 27.8 %collective-permute-start.4 = (f32[32,512]{1,0:T(8,128)S(1)}, f32[32,512]{1,0:T(8,128)}, u32[]{:S(2)}, u32[]{:S(2)}) collective-permute-start(f32[32,512]{1,0:T(8,128)S(1)} %fusion), channel_id=1, source_target_pairs={{0,40},{8,48},{16,56},{24,64},{32,72},{40,80},{48,88},{56,96},{64,... | collective-permute-start | bytes 196616
  198.5 25.9 %collective-permute-start.3 = (f32[32,512]{1,0:T(8,128)S(1)}, f32[32,512]{1,0:T(8,128)}, u32[]{:S(2)}, u32[]{:S(2)}) collective-permute-start(f32[32,512]{1,0:T(8,128)S(1)} %fusion), channel_id=1, source_target_pairs={{0,32},{8,40},{16,48},{24,56},{32,64},{40,72},{48,80},{56,88},{64,... | collective-permute-start | bytes 196616
  209.3 12.4 %copy-start.7 = (f32[28,512]{1,0:T(8,128)}, f32[28,512]{1,0:T(8,128)S(1)}, u32[]{:S(2)}) copy-start(f32[28,512]{1,0:T(8,128)S(1)} %collective-permute-done.7) | copy-start | bytes 172036
  209.3 15.1 %collective-permute-start.2 = (f32[32,512]{1,0:T(8,128)S(1)}, f32[32,512]{1,0:T(8,128)}, u32[]{:S(2)}, u32[]{:S(2)}) collective-permute-start(f32[32,512]{1,0:T(8,128)S(1)} %fusion), channel_id=1, source_target_pairs={{0,24},{8,32},{16,40},{24,48},{32,56},{40,64},{48,72},{56,80},{64,... | collective-permute-start | bytes 196616
  211.2 8.3 %copy-start.5 = (f32[32,512]{1,0:T(8,128)}, f32[32,512]{1,0:T(8,128)S(1)}, u32[]{:S(2)}) copy-start(f32[32,512]{1,0:T(8,128)S(1)} %collective-permute-done.6) | copy-start | bytes 196612
  211.2 13.2 %collective-permute-start.1 = (f32[32,512]{1,0:T(8,128)S(1)}, f32[32,512]{1,0:T(8,128)}, u32[]{:S(2)}, u32[]{:S(2)}) collective-permute-start(f32[32,512]{1,0:T(8,128)S(1)} %fusion), channel_id=1, source_target_pairs={{0,16},{8,24},{16,32},{24,40},{32,48},{40,56},{48,64},{56,72},{64,... | collective-permute-start | bytes 196616
  219.5 2.2 copy-start.6
  219.5 4.9 %collective-permute-start = (f32[32,512]{1,0:T(8,128)S(1)}, f32[32,512]{1,0:T(8,128)}, u32[]{:S(2)}, u32[]{:S(2)}) collective-permute-start(f32[32,512]{1,0:T(8,128)S(1)} %fusion), channel_id=1, source_target_pairs={{0,8},{8,16},{16,24},{24,32},{32,40},{40,48},{48,56},{56,64},{64,7... | collective-permute-start | bytes 196616
  239.2 89.0 %copy-start.3 = (f32[28,512]{1,0:T(8,128)}, f32[28,512]{1,0:T(8,128)S(1)}, u32[]{:S(2)}) copy-start(f32[28,512]{1,0:T(8,128)S(1)} %fusion.3) | copy-start | bytes 172036
Sparse Core Ops, SparseCore 0:
  240.0 84.4 all-gather.2
where the time goes:
time: 336 us; the launch traced here: 335 us
  blocking collectives  178 us (53%)
  waiting for transfers between devices  84.7 us (25%)
  starting transfers between devices  29 us (9%)
  local copies, waits for them, and re-layouts  19 us (6%)
  between operations  15.6 us (5%)
  matrix products  7.24 us (2%)
    unnamed x1, blocking collectives  178 us
    all_gather x1, waiting for transfers between devices, local(): weights = lax.all_gather(own_weights, 'dp', axis=0, tiled=True)  84.6 us
    unnamed x8, starting transfers between devices  28.9 us
    unnamed x20, local copies, waits for them, and re-layouts  19 us
  transfers between devices with their start and end apart: 9, of which 1 were waited for; matrix products, arithmetic and copies ran while one was open for 0% of the time, Pallas kernels for 0%

commit v1 on v0

--- a/solution.py
+++ b/solution.py
@@ -40,7 +40,9 @@
         + 0.1 * master
     )
     own_weights = (master - 0.0003 * update).astype(jnp.bfloat16)
-    weights = lax.all_gather(own_weights, "dp", axis=0, tiled=True)
+    weights = jnp.concatenate(
+        lax.all_to_all(jnp.stack([own_weights] * lax.axis_size("dp")), "dp", 0, 0), axis=0
+    )
     return (weights, update)
 
 

time: 336 us -> 308 us (0.917)
  the two profiles are of different devices: /device:TPU:1 before, /device:TPU:45 now
where the time goes in v1:
time: 308 us; the launch traced here: 307 us
  blocking collectives  220 us (71%)
  starting transfers between devices  56.8 us (18%)
  local copies, waits for them, and re-layouts  19.3 us (6%)
  matrix products  7.89 us (3%)
    unnamed x1, blocking collectives  142 us
    all_to_all x1, blocking collectives, local(): lax.all_to_all(jnp.stack([own_weights] * lax.axis_size('dp')), 'dp', 0, 0)  77.8 us
    unnamed x8, starting transfers between devices  56.8 us
    unnamed x17, local copies, waits for them, and re-layouts  15.3 us
  transfers between devices with their start and end apart: 8, of which 0 were waited for; matrix products, arithmetic and copies ran while one was open for 0% of the time, Pallas kernels for 0%

profile of v1, /device:TPU:45, one launch (start us, length us, event | category | flops | bytes accessed | tf_op | source)
XLA Modules:
  0.0 306.8 jit_solution(10449679138586649896)
XLA Ops:
  0.6 0.0 copy-start
  0.6 0.9 fusion.32
  1.5 0.8 copy-done
  2.3 5.6 %fusion.1 = f32[1792,512]{1,0:T(8,128)} fusion(bf16[512,512]{1,0:T(8,128)(2,1)} %constant.26.clone.1, bf16[640,1792]{1,0:T(8,128)(2,1)S(1)} %copy-done, bf16[640,512]{1,0:T(8,128)(2,1)} %param.8, bf16[512]{0:T(512)(128)(2,1)S(1)} %get-tuple-element.3), kind=kOutput, calls=%fused_computation.1 | convolution fusion | flops 2117599232 | bytes 7144448 | tf_op jit(solution)/shard_map/dot_general | solution.py:29
  7.9 141.9 %fusion = f32[32,512]{1,0:T(8,128)S(1)} fusion(f32[1792,512]{1,0:T(8,128)} %fusion.1), kind=kCustom, calls=%all-reduce-scatter | all-reduce-scatter fusion | flops 1048577 | bytes 3737600
  149.9 6.5 %collective-permute-start.6 = (f32[32,512]{1,0:T(8,128)S(1)}, f32[32,512]{1,0:T(8,128)S(1)}, u32[]{:S(2)}, u32[]{:S(2)}) collective-permute-start(f32[32,512]{1,0:T(8,128)S(1)} %fusion), channel_id=1, source_target_pairs={{0,56},{8,64},{16,72},{24,80},{32,88},{40,96},{48,104},{56,112},{6... | collective-permute-start | bytes 196616
  156.4 7.9 %collective-permute-start.5 = (f32[32,512]{1,0:T(8,128)S(1)}, f32[32,512]{1,0:T(8,128)S(1)}, u32[]{:S(2)}, u32[]{:S(2)}) collective-permute-start(f32[32,512]{1,0:T(8,128)S(1)} %fusion), channel_id=1, source_target_pairs={{0,48},{8,56},{16,64},{24,72},{32,80},{40,88},{48,96},{56,104},{64... | collective-permute-start | bytes 196616
  164.3 31.0 %collective-permute-start.7 = (f32[28,512]{1,0:T(8,128)S(1)}, f32[28,512]{1,0:T(8,128)S(1)}, u32[]{:S(2)}, u32[]{:S(2)}) collective-permute-start(f32[28,512]{1,0:T(8,128)S(1)} %slice), channel_id=1, source_target_pairs={{0,64},{8,72},{16,80},{24,88},{32,96},{40,104},{48,112},{56,120},{... | collective-permute-start | bytes 172040
  195.4 1.9 collective-permute-start.4
  197.3 1.9 collective-permute-start.3
  199.2 0.0 copy-start.6
  199.3 3.0 collective-permute-start.2
  202.3 0.0 collective-permute-done.6
  202.3 1.9 collective-permute-start.1
  204.3 0.0 collective-permute-done.5
  204.3 2.5 collective-permute-start
  207.5 1.3 dynamic-slice.4
  209.5 0.0 collective-permute-done.4
  209.5 0.0 collective-permute-done.1
  209.5 13.2 %concatenate = f32[284,512]{1,0:T(8,128)} concatenate(f32[28,512]{1,0:T(8,128)} %copy-done.6, f32[32,512]{1,0:T(8,128)} %copy-done.4, f32[32,512]{1,0:T(8,128)} %copy-done.5, f32[32,512]{1,0:T(8,128)} %collective-permute-done.4, f32[32,512]{1,0:T(8,128)} %collective-permute-done.3, f32[32,512]{1,0:T(8,128)} %collective-permute-done.2, f32[32,512]{1,0:T(8,128)} %collective-permute-done.1, ...), dimensions={0} | concatenate | bytes 1163264
  222.7 2.3 subtract_convert_fusion
  225.0 0.2 stack.2
  225.2 77.8 %all_to_all.5 = bf16[64,28,512]{2,1,0:T(8,128)(2,1)} all-to-all(bf16[64,28,512]{2,1,0:T(8,128)(2,1)S(1)} %stack.2), channel_id=1, replica_groups=mesh['dp'=64,'mp'=8] {'dp'}, dimensions={0} | all-to-all | bytes 3670016 | tf_op jit(solution)/shard_map/all_to_all | solution.py:44
  303.1 3.7 %reshape.20 = bf16[1792,512]{1,0:T(8,128)(2,1)} reshape(bf16[64,28,512]{2,1,0:T(8,128)(2,1)} %all_to_all.5) | data formatting | bytes 3670016 | tf_op jit(solution)/shard_map/reshape | solution.py:43
  (16 shorter events, 0.0 us)
Async XLA Ops:
  0.6 1.7 copy-start
  7.9 214.8 %copy-start.1 = (f32[512,512]{1,0:T(8,128)S(1)}, f32[512,512]{1,0:T(8,128)}, u32[]{:S(2)}) copy-start(f32[512,512]{1,0:T(8,128)} %constant.35.clone.1) | copy-start | bytes 3145732
  7.9 214.8 %copy-start.2 = (f32[28,512]{1,0:T(8,128)S(1)}, f32[28,512]{1,0:T(8,128)}, u32[]{:S(2)}) copy-start(f32[28,512]{1,0:T(8,128)} %param.9) | copy-start | bytes 172036
  7.9 214.8 %copy-start.3 = (f32[28,512]{1,0:T(8,128)S(1)}, f32[28,512]{1,0:T(8,128)}, u32[]{:S(2)}) copy-start(f32[28,512]{1,0:T(8,128)} %param.11) | copy-start | bytes 172036
  149.9 52.4 %collective-permute-start.6 = (f32[32,512]{1,0:T(8,128)S(1)}, f32[32,512]{1,0:T(8,128)S(1)}, u32[]{:S(2)}, u32[]{:S(2)}) collective-permute-start(f32[32,512]{1,0:T(8,128)S(1)} %fusion), channel_id=1, source_target_pairs={{0,56},{8,64},{16,72},{24,80},{32,88},{40,96},{48,104},{56,112},{6... | collective-permute-start | bytes 196616
  156.4 47.9 %collective-permute-start.5 = (f32[32,512]{1,0:T(8,128)S(1)}, f32[32,512]{1,0:T(8,128)S(1)}, u32[]{:S(2)}, u32[]{:S(2)}) collective-permute-start(f32[32,512]{1,0:T(8,128)S(1)} %fusion), channel_id=1, source_target_pairs={{0,48},{8,56},{16,64},{24,72},{32,80},{40,88},{48,96},{56,104},{64... | collective-permute-start | bytes 196616
  164.3 34.9 %collective-permute-start.7 = (f32[28,512]{1,0:T(8,128)S(1)}, f32[28,512]{1,0:T(8,128)S(1)}, u32[]{:S(2)}, u32[]{:S(2)}) collective-permute-start(f32[28,512]{1,0:T(8,128)S(1)} %slice), channel_id=1, source_target_pairs={{0,64},{8,72},{16,80},{24,88},{32,96},{40,104},{48,112},{56,120},{... | collective-permute-start | bytes 172040
  195.4 14.1 %collective-permute-start.4 = (f32[32,512]{1,0:T(8,128)S(1)}, f32[32,512]{1,0:T(8,128)}, u32[]{:S(2)}, u32[]{:S(2)}) collective-permute-start(f32[32,512]{1,0:T(8,128)S(1)} %fusion), channel_id=1, source_target_pairs={{0,40},{8,48},{16,56},{24,64},{32,72},{40,80},{48,88},{56,96},{64,... | collective-permute-start | bytes 196616
  197.3 12.2 %collective-permute-start.3 = (f32[32,512]{1,0:T(8,128)S(1)}, f32[32,512]{1,0:T(8,128)}, u32[]{:S(2)}, u32[]{:S(2)}) collective-permute-start(f32[32,512]{1,0:T(8,128)S(1)} %fusion), channel_id=1, source_target_pairs={{0,32},{8,40},{16,48},{24,56},{32,64},{40,72},{48,80},{56,88},{64,... | collective-permute-start | bytes 196616
  199.2 7.5 %copy-start.6 = (f32[28,512]{1,0:T(8,128)}, f32[28,512]{1,0:T(8,128)S(1)}, u32[]{:S(2)}) copy-start(f32[28,512]{1,0:T(8,128)S(1)} %collective-permute-done.7) | copy-start | bytes 172036
  199.3 10.2 %collective-permute-start.2 = (f32[32,512]{1,0:T(8,128)S(1)}, f32[32,512]{1,0:T(8,128)}, u32[]{:S(2)}, u32[]{:S(2)}) collective-permute-start(f32[32,512]{1,0:T(8,128)S(1)} %fusion), channel_id=1, source_target_pairs={{0,24},{8,32},{16,40},{24,48},{32,56},{40,64},{48,72},{56,80},{64,... | collective-permute-start | bytes 196616
  202.3 2.0 copy-start.4
  202.3 7.2 %collective-permute-start.1 = (f32[32,512]{1,0:T(8,128)S(1)}, f32[32,512]{1,0:T(8,128)}, u32[]{:S(2)}, u32[]{:S(2)}) collective-permute-start(f32[32,512]{1,0:T(8,128)S(1)} %fusion), channel_id=1, source_target_pairs={{0,16},{8,24},{16,32},{24,40},{32,48},{40,56},{48,64},{56,72},{64,... | collective-permute-start | bytes 196616
  204.3 2.5 copy-start.5
  204.3 5.2 %collective-permute-start = (f32[32,512]{1,0:T(8,128)S(1)}, f32[32,512]{1,0:T(8,128)}, u32[]{:S(2)}, u32[]{:S(2)}) collective-permute-start(f32[32,512]{1,0:T(8,128)S(1)} %fusion), channel_id=1, source_target_pairs={{0,8},{8,16},{16,24},{24,32},{32,40},{40,48},{48,56},{56,64},{64,7... | collective-permute-start | bytes 196616
